TPU v7x, 256 devices: a whole 4x4x8 slice. The times are simulated.
256 devices in a mesh: lon: 64 (over y, x_hi, z), lat: 4 (over x_lo, core).
Axes of the slice: x: 4 (x_hi: 2, x_lo: 2; x = x_hi * 2 + x_lo), y: 4, z: 8, core: 2. Of those that a mesh axis runs over, the one named last changes fastest.
Arguments:
- queries: bfloat16 [64, 1024, 1024], P('lat', 'lon'), may hold values from -8 to 8
- key_vectors: bfloat16 [64, 1024, 1024], P('lat', 'lon'), may hold values from -8 to 8
- value_vectors: bfloat16 [64, 1024, 1024], P('lat', 'lon'), may hold values from -6 to 6
- grad_out: bfloat16 [64, 1024, 1024], P('lat', 'lon'), may hold values from -6 to 6
- key_mask: int32 [64, 1024], P('lat', 'lon'), may hold values 0 or 1
- block_lists: int32 [64, 3], P('lon'), may hold values from 0 to 63, as said below
Outputs:
- attended: bfloat16 [64, 1024, 1024], P('lat', 'lon')
- grad_queries: bfloat16 [64, 1024, 1024], P('lat', 'lon')
- grad_keys: bfloat16 [64, 1024, 1024], P('lat', 'lon')
- grad_values: bfloat16 [64, 1024, 1024], P('lat', 'lon')
Inputs may be any that keep to these rules, and one draw needn't show every extreme that they name: `block_lists`: row b names 3 different blocks: b itself, one block exactly 3 blocks from b around the loop of 64 blocks, and one block nearer to b than that, in any order.
All inputs are finite; a program needn't handle non-finite values. No bound on the sum of `key_mask` on one device may be relied on, other than what follows from the above.
Results may differ from a plain program's by a relative error of at most 0.013.
The roundings to bfloat16 on the way count: a program that leaves them out, or rounds other values in their place, can miss the bound.
Values may be sent and summed in bfloat16 or wider, within the bound.
A program may use at most 128 MiB of HBM per device.

v0:
```python
import functools

import jax
import jax.numpy as jnp
import numpy as np
from jax import lax
from jax.experimental import pallas as pl
from jax.experimental.pallas import tpu as pltpu
from jax.sharding import PartitionSpec as P

HEAD = 64
NB_HEADS = 12
RAD = 6
RANGE = 3
SIDE = 16
CELLS = SIDE * SIDE
WCH = NB_HEADS * HEAD
PAIR = 2 * HEAD
PAIRS = WCH // PAIR
XPAIRS = 2
STRIP = RAD * SIDE
LEFT = CELLS
RIGHT = CELLS + STRIP
EDGE = CELLS + 2 * STRIP
CORNER = EDGE + STRIP
KEYS = CORNER + STRIP
NSLOT = 2 * RANGE + 1
GROUP = 64
GROUPS = CELLS // GROUP
NEG = -1e30
SCALE = HEAD**-0.5
BF = jnp.bfloat16
F32 = jnp.float32
NEAR = [(o, 0) for o in (1, -1, 2, -2, 3, -3)] + [(o, a) for a in (-1, 1) for o in (0, 1, -1)]


def key_places(tile):
    rows = np.full(KEYS, 1000)
    cols = np.full(KEYS, 1000)
    own = np.arange(CELLS)
    rows[:CELLS], cols[:CELLS] = own // SIDE, own % SIDE
    strip = np.arange(STRIP)
    rows[LEFT:RIGHT], cols[LEFT:RIGHT] = strip % SIDE, strip // SIDE - RAD
    rows[RIGHT:EDGE], cols[RIGHT:EDGE] = strip % SIDE, strip // SIDE + SIDE
    first = -RAD if tile == 0 else SIDE
    rows[EDGE:CORNER], cols[EDGE:CORNER] = first + strip // SIDE, strip % SIDE
    for side in range(2):
        for c in range(RAD):
            for r in range(RAD):
                at = CORNER + side * RAD * RAD + c * RAD + r
                rows[at] = first + r
                cols[at] = c - RAD if side == 0 else c + SIDE
    return rows, cols


def tables():
    window = np.zeros((2, KEYS, 128), np.float32)
    lane = np.arange(128)
    for tile in range(2):
        rows, cols = key_places(tile)
        q_row, q_col = lane // SIDE + 8 * tile, lane % SIDE
        dr = rows[:, None] - q_row[None, :]
        dc = cols[:, None] - q_col[None, :]
        window[tile] = ((np.abs(dr) <= RAD) & (np.abs(dc) <= RAD)) + 1.0 * ((dr == 0) & (dc == 0))
    slot = np.arange(NSLOT * GROUP)
    cell = slot % GROUP
    query = lane % GROUP
    axial = (cell[:, None] // SIDE == query[None, :] // SIDE) + 1.0 * (
        (cell[:, None] == query[None, :]) & (slot[:, None] // GROUP == RANGE)
    )
    strips = np.zeros((2 * STRIP, CELLS), np.float32)
    for c in range(RAD):
        for r in range(SIDE):
            strips[c * SIDE + r, r * SIDE + SIDE - RAD + c] = 1
            strips[STRIP + c * SIDE + r, r * SIDE + c] = 1
    corners = np.zeros((2 * STRIP, 2 * STRIP), np.float32)
    for side in range(2):
        for c in range(RAD):
            for r in range(RAD):
                at = side * RAD * RAD + c * RAD + r
                corners[at, side * STRIP + c * SIDE + r] = 1
                corners[STRIP + at, side * STRIP + c * SIDE + SIDE - RAD + r] = 1
    return [jnp.asarray(t, BF) for t in (window, axial, strips, strips.T, corners, corners.T)]


def mm(a, b):
    return jnp.dot(a, b, preferred_element_type=F32)


def mm_nt(a, b):
    return lax.dot_general(a, b, (((1,), (1,)), ((), ())), preferred_element_type=F32)


def mm_tn(a, b):
    return lax.dot_general(a, b, (((0,), (0,)), ((), ())), preferred_element_type=F32)


def stacked_heads(block):
    low = lax.broadcasted_iota(jnp.int32, block.shape, 1) < HEAD
    zero = jnp.zeros_like(block)
    return jnp.concatenate([jnp.where(low, block, zero), jnp.where(low, zero, block)], axis=0)


def probabilities(scores, dprob):
    top = jnp.max(scores, axis=0, keepdims=True)
    expo = jnp.exp(scores - top)
    probs = expo * (1.0 / jnp.sum(expo, axis=0, keepdims=True))
    delta = jnp.sum(probs * dprob, axis=0, keepdims=True)
    return probs.astype(BF), (probs * (dprob - delta)).astype(BF)


def kernel(
    nlon, nlat,
    q_ref, k_ref, v_ref, g_ref, flag_ref, listed_ref,
    near_ref, row_ref, strips_ref, strips_t_ref, corners_ref, corners_t_ref,
    out_ref, gq_ref, gk_ref, gv_ref,
    flags, columns, bias, xbias, kv, strip_out, corner_out, xkv,
    acc, sides, edge_out, edge_in, side_out, side_in, gx, hop_out, hop_in,
    flag_s, flag_r, strip_s, strip_r, edge_s, edge_r, corner_s, corner_r, ax_s, ax_r,
    bedge_s, bedge_r, bside_s, bside_r, hop_s, hop_r,
):
    lon = lax.axis_index("lon")
    lat = lax.axis_index("lat")
    has_up = lat > 0
    has_down = lat < nlat - 1

    def device(dlon, dlat):
        return {"lon": lax.rem(lon + dlon + nlon, nlon), "lat": lax.rem(lat + dlat + nlat, nlat)}

    def remote(src, dst, send, recv, dlon, dlat):
        return pltpu.make_async_remote_copy(
            src_ref=src, dst_ref=dst, send_sem=send, recv_sem=recv,
            device_id=device(dlon, dlat), device_id_type=pl.DeviceIdType.MESH,
        )

    barrier = pltpu.get_barrier_semaphore()
    for dlon, dlat in NEAR:
        pl.semaphore_signal(barrier, inc=1, device_id=device(dlon, dlat), device_id_type=pl.DeviceIdType.MESH)

    flags[RANGE] = flag_ref[...]
    for part, ref in enumerate((k_ref, v_ref)):
        cells = ref[:, :WCH]
        for tile in range(2):
            kv[tile, part, 0:CELLS] = cells
        strip_out[part] = mm(strips_ref[...], cells).astype(BF)
        for pair in range(XPAIRS):
            at = (2 * pair + part) * PAIR
            xkv[RANGE, :, at:at + PAIR] = ref[:, WCH + pair * PAIR:WCH + (pair + 1) * PAIR]
    for tile, there in enumerate((has_up, has_down)):
        @pl.when(jnp.logical_not(there))
        def _():
            kv[tile, :, EDGE:KEYS] = jnp.zeros((2, KEYS - EDGE, WCH), BF)
            edge_in[tile] = jnp.zeros(edge_in.shape[1:], BF)

    pl.semaphore_wait(barrier, len(NEAR))

    def flag_copy(index):
        dlon, dlat = NEAR[index]
        slot = {0: RANGE, -1: 11, 1: 8}[dlat] - dlon
        return remote(flags.at[RANGE], flags.at[slot], flag_s.at[index], flag_r.at[slot], dlon, dlat)

    def strip_copy(way):
        return remote(
            strip_out.at[:, pl.ds(way * STRIP, STRIP)], kv.at[0, :, pl.ds(LEFT + way * STRIP, STRIP)],
            strip_s.at[way], strip_r.at[way], 1 - 2 * way, 0,
        )

    def edge_copy(way):
        return remote(
            kv.at[0, :, pl.ds(way * (CELLS - STRIP), STRIP)], kv.at[1 - way, :, pl.ds(EDGE, STRIP)],
            edge_s.at[way], edge_r.at[way], 0, 2 * way - 1,
        )

    def corner_copy(way):
        return remote(
            corner_out.at[:, pl.ds(way * STRIP, STRIP)], kv.at[1 - way, :, pl.ds(CORNER, STRIP)],
            corner_s.at[way], corner_r.at[way], 0, 2 * way - 1,
        )

    def ax_copy(way, step):
        sign = 1 - 2 * way
        return remote(
            xkv.at[RANGE - sign * step], xkv.at[RANGE - sign * (step + 1)],
            ax_s.at[way, step], ax_r.at[way, step], sign, 0,
        )

    def edge_back(way, pair):
        lanes = pl.ds(pl.multiple_of(pair * PAIR, PAIR), PAIR)
        return remote(
            edge_out.at[way, :, :, lanes], edge_in.at[1 - way, :, :, lanes],
            bedge_s.at[way, pair], bedge_r.at[way, pair], 0, 2 * way - 1,
        )

    def side_back(way, pair):
        lanes = pl.ds(pl.multiple_of(pair * PAIR, PAIR), PAIR)
        rows = pl.ds(way * STRIP, STRIP)
        return remote(
            side_out.at[:, rows, lanes], side_in.at[:, rows, lanes],
            bside_s.at[way, pair], bside_r.at[way, pair], 2 * way - 1, 0,
        )

    def hop_back(way, step, pair):
        lanes = pl.ds(pair * 2 * PAIR, 2 * PAIR)
        return remote(
            hop_out.at[way, step, :, lanes], hop_in.at[way, step, :, lanes],
            hop_s.at[way, step, pair], hop_r.at[way, step, pair], 1 - 2 * way, 0,
        )

    def vertical(make, sending):
        @pl.when(has_up)
        def _():
            make(0 if sending else 1)

        @pl.when(has_down)
        def _():
            make(1 if sending else 0)

    for index in range(len(NEAR)):
        flag_copy(index).start()
    for way in range(2):
        strip_copy(way).start()
    vertical(lambda way: edge_copy(way).start(), True)
    for way in range(2):
        ax_copy(way, 0).start()

    for index in range(len(NEAR)):
        flag_copy(index).wait_recv()
    for slot in range(13):
        for half in range(2):
            row = jnp.broadcast_to(flags[slot, half:half + 1, :], (128, 128))
            columns[slot, half * 128:(half + 1) * 128] = row.T.astype(BF)

    def sides_of(left, right):
        return jnp.concatenate(
            [mm(strips_ref[0:STRIP], columns[left]), mm(strips_ref[STRIP:], columns[right])], axis=0
        )

    own_flags = columns[RANGE].astype(F32)
    side_flags = sides_of(RANGE - 1, RANGE + 1)
    for tile, there in enumerate((has_up, has_down)):
        base = 7 + 3 * tile
        lives = jnp.where(there, 1.0, 0.0)
        first = CELLS - STRIP if tile == 0 else 0
        edge_flags = columns[base + 1, first:first + STRIP].astype(F32)
        turn = corners_ref[STRIP:] if tile == 0 else corners_ref[0:STRIP]
        corner_flags = mm(turn, sides_of(base, base + 2).astype(BF))
        serves = jnp.concatenate([own_flags, side_flags, edge_flags * lives, corner_flags * lives], axis=0)
        bias[tile] = jnp.where(near_ref[tile].astype(F32) + serves > 1.5, 0.0, NEG)
    for group in range(GROUPS):
        serves = jnp.concatenate(
            [
                columns[slot, group * GROUP:(group + 1) * GROUP].astype(F32) * listed_ref[slot:slot + 1, :]
                for slot in range(NSLOT)
            ],
            axis=0,
        )
        xbias[group] = jnp.where(row_ref[...].astype(F32) + serves > 1.5, 0.0, NEG)

    for way in range(2):
        strip_copy(way).wait_recv()
    for part in range(2):
        strip = kv[0, part, LEFT:EDGE]
        kv[1, part, LEFT:EDGE] = strip
        corner_out[part] = mm(corners_ref[...], strip).astype(BF)
    vertical(lambda way: corner_copy(way).start(), True)
    vertical(lambda way: edge_copy(way).wait_recv(), False)
    vertical(lambda way: corner_copy(way).wait_recv(), False)

    def send_sides(pair):
        lanes = pl.ds(pl.multiple_of(pair * PAIR, PAIR), PAIR)
        vertical(lambda way: edge_back(way, pair).wait_recv(), False)
        for part in range(2):
            found = jnp.concatenate(
                [edge_in[0, part, STRIP:2 * STRIP, lanes], edge_in[1, part, STRIP:2 * STRIP, lanes]], axis=0
            )
            side_out[part, :, lanes] = (sides[part, :, lanes] + mm(corners_t_ref[...], found)).astype(BF)
        for way in range(2):
            side_back(way, pair).start()

    def window_pair(pair, carry):
        lanes = pl.ds(pl.multiple_of(pair * PAIR, PAIR), PAIR)
        grads = []
        for tile in range(2):
            rows = slice(tile * 128, (tile + 1) * 128)
            queries = stacked_heads(q_ref[rows, lanes] * jnp.asarray(SCALE, BF))
            cotangents = stacked_heads(g_ref[rows, lanes])
            keys = kv[tile, 0, :, lanes]
            values = kv[tile, 1, :, lanes]
            penalty = bias[tile]
            scores = mm_nt(keys, queries) + jnp.concatenate([penalty, penalty], axis=1)
            probs, dscore = probabilities(scores, mm_nt(values, cotangents))
            attended = mm_tn(values, probs)
            grad_q = mm_tn(keys, dscore)
            for result, ref, factor in ((attended, out_ref, 1.0), (grad_q, gq_ref, SCALE)):
                both = jnp.concatenate([result[0:HEAD, 0:128], result[HEAD:, 128:]], axis=0)
                ref[rows, lanes] = (both.T * factor).astype(BF)
            grads.append((mm(dscore, queries), mm(probs, cotangents)))
        for part in range(2):
            first, second = grads[0][part], grads[1][part]
            acc[part, :, lanes] = first[0:CELLS] + second[0:CELLS]
            sides[part, :, lanes] = first[LEFT:EDGE] + second[LEFT:EDGE]
            edge_out[0, part, :, lanes] = first[EDGE:].astype(BF)
            edge_out[1, part, :, lanes] = second[EDGE:].astype(BF)
        vertical(lambda way: edge_back(way, pair).start(), True)

        for step in range(2):
            @pl.when(pair == 2 * step + 1)
            def _():
                for way in range(2):
                    ax_copy(way, step).wait_recv()
                    ax_copy(way, step + 1).start()

        @pl.when(pair > 0)
        def _():
            send_sides(pair - 1)

        return carry

    lax.fori_loop(0, PAIRS, window_pair, 0)
    send_sides(PAIRS - 1)
    for way in range(2):
        ax_copy(way, 2).wait_recv()

    for pair in range(XPAIRS):
        lanes = slice(WCH + pair * PAIR, WCH + (pair + 1) * PAIR)
        key_lanes = slice(2 * pair * PAIR, (2 * pair + 1) * PAIR)
        value_lanes = slice((2 * pair + 1) * PAIR, (2 * pair + 2) * PAIR)

        def axial_group(group, carry):
            cells = pl.ds(pl.multiple_of(group * GROUP, GROUP), GROUP)
            queries = stacked_heads(q_ref[cells, lanes] * jnp.asarray(SCALE, BF))
            cotangents = stacked_heads(g_ref[cells, lanes])
            keys = xkv[:, cells, key_lanes].reshape(NSLOT * GROUP, PAIR)
            values = xkv[:, cells, value_lanes].reshape(NSLOT * GROUP, PAIR)
            scores = mm_nt(keys, queries) + xbias[group]
            probs, dscore = probabilities(scores, mm_nt(values, cotangents))
            attended = mm_tn(probs, values)
            grad_q = mm_tn(dscore, keys)
            low = lax.broadcasted_iota(jnp.int32, (GROUP, PAIR), 1) < HEAD
            out_ref[cells, lanes] = jnp.where(low, attended[0:GROUP], attended[GROUP:]).astype(BF)
            gq_ref[cells, lanes] = (jnp.where(low, grad_q[0:GROUP], grad_q[GROUP:]) * SCALE).astype(BF)
            gx[:, cells, key_lanes] = mm(dscore, queries).reshape(NSLOT, GROUP, PAIR)
            gx[:, cells, value_lanes] = mm(probs, cotangents).reshape(NSLOT, GROUP, PAIR)
            return carry

        lax.fori_loop(0, GROUPS, axial_group, 0)
        both = slice(2 * pair * PAIR, (2 * pair + 2) * PAIR)
        for way in range(2):
            hop_out[way, 0, :, both] = gx[2 * RANGE * (1 - way), :, both].astype(BF)
            hop_back(way, 0, pair).start()

    for step in range(1, RANGE):
        for pair in range(XPAIRS):
            both = slice(2 * pair * PAIR, (2 * pair + 2) * PAIR)
            for way in range(2):
                slot = 2 * RANGE - step if way == 0 else step
                hop_back(way, step - 1, pair).wait_recv()
                total = gx[slot, :, both] + hop_in[way, step - 1, :, both].astype(F32)
                hop_out[way, step, :, both] = total.astype(BF)
                hop_back(way, step, pair).start()

    for pair in range(PAIRS):
        for way in range(2):
            side_back(way, pair).wait_recv()
    for part, ref in enumerate((gk_ref, gv_ref)):
        total = acc[part] + mm(strips_t_ref[...], side_in[part])
        ref[0:STRIP, :WCH] = (total[0:STRIP] + edge_in[0, part, 0:STRIP].astype(F32)).astype(BF)
        ref[STRIP:CELLS - STRIP, :WCH] = total[STRIP:CELLS - STRIP].astype(BF)
        ref[CELLS - STRIP:, :WCH] = (total[CELLS - STRIP:] + edge_in[1, part, 0:STRIP].astype(F32)).astype(BF)

    for pair in range(XPAIRS):
        lanes = slice(WCH + pair * PAIR, WCH + (pair + 1) * PAIR)
        for way in range(2):
            hop_back(way, RANGE - 1, pair).wait_recv()
        for part, ref in enumerate((gk_ref, gv_ref)):
            at = slice((2 * pair + part) * PAIR, (2 * pair + part + 1) * PAIR)
            total = gx[RANGE, :, at]
            for way in range(2):
                total = total + hop_in[way, RANGE - 1, :, at].astype(F32)
            ref[:, lanes] = total.astype(BF)

    for index in range(len(NEAR)):
        flag_copy(index).wait_send()
    for way in range(2):
        strip_copy(way).wait_send()
        for step in range(RANGE):
            ax_copy(way, step).wait_send()
            for pair in range(XPAIRS):
                hop_back(way, step, pair).wait_send()
        for pair in range(PAIRS):
            side_back(way, pair).wait_send()
    vertical(lambda way: edge_copy(way).wait_send(), True)
    vertical(lambda way: corner_copy(way).wait_send(), True)
    for pair in range(PAIRS):
        vertical(lambda way: edge_back(way, pair).wait_send(), True)


def per_device(nlon, nlat, queries, key_vectors, value_vectors, grad_out, key_mask, block_lists):
    shape = queries.shape
    flat = [x.reshape(CELLS, shape[-1]) for x in (queries, key_vectors, value_vectors, grad_out)]
    flag = jnp.pad((key_mask > 0).astype(F32).reshape(2, 128), ((0, 6), (0, 0)))
    offset = (block_lists[0] - lax.axis_index("lon") + RANGE + nlon) % nlon
    listed = jnp.any(jnp.arange(8)[:, None] == offset[None, :], axis=1)
    listed = jnp.broadcast_to(listed[:, None], (8, 128)).astype(F32)
    vmem = pl.BlockSpec(memory_space=pltpu.VMEM)
    dma = lambda *s: pltpu.SemaphoreType.DMA(s)
    outs = pl.pallas_call(
        functools.partial(kernel, nlon, nlat),
        out_shape=[jax.ShapeDtypeStruct((CELLS, shape[-1]), BF)] * 4,
        in_specs=[vmem] * 12,
        out_specs=[vmem] * 4,
        scratch_shapes=[
            pltpu.VMEM((13, 8, 128), F32),
            pltpu.VMEM((13, CELLS, 128), BF),
            pltpu.VMEM((2, KEYS, 128), F32),
            pltpu.VMEM((GROUPS, NSLOT * GROUP, 128), F32),
            pltpu.VMEM((2, 2, KEYS, WCH), BF),
            pltpu.VMEM((2, 2 * STRIP, WCH), BF),
            pltpu.VMEM((2, 2 * STRIP, WCH), BF),
            pltpu.VMEM((NSLOT, CELLS, 2 * XPAIRS * PAIR), BF),
            pltpu.VMEM((2, CELLS, WCH), F32),
            pltpu.VMEM((2, 2 * STRIP, WCH), F32),
            pltpu.VMEM((2, 2, 2 * STRIP, WCH), BF),
            pltpu.VMEM((2, 2, 2 * STRIP, WCH), BF),
            pltpu.VMEM((2, 2 * STRIP, WCH), BF),
            pltpu.VMEM((2, 2 * STRIP, WCH), BF),
            pltpu.VMEM((NSLOT, CELLS, 2 * XPAIRS * PAIR), F32),
            pltpu.VMEM((2, RANGE, CELLS, 2 * XPAIRS * PAIR), BF),
            pltpu.VMEM((2, RANGE, CELLS, 2 * XPAIRS * PAIR), BF),
            dma(len(NEAR)), dma(13), dma(2), dma(2), dma(2), dma(2), dma(2), dma(2),
            dma(2, RANGE), dma(2, RANGE), dma(2, PAIRS), dma(2, PAIRS), dma(2, PAIRS), dma(2, PAIRS),
            dma(2, RANGE, XPAIRS), dma(2, RANGE, XPAIRS),
        ],
        compiler_params=pltpu.CompilerParams(
            collective_id=0, has_side_effects=True, vmem_limit_bytes=52 * 1024 * 1024
        ),
        cost_estimate=pl.CostEstimate(flops=4_000_000_000, bytes_accessed=5_000_000, transcendentals=3_000_000),
    )(*flat, flag, listed, *tables())
    return tuple(x.reshape(shape) for x in outs)


def solution(mesh):
    cells = P("lat", "lon", None)
    return jax.shard_map(
        functools.partial(per_device, mesh.shape["lon"], mesh.shape["lat"]),
        mesh=mesh,
        in_specs=(cells, cells, cells, cells, P("lat", "lon"), P("lon", None)),
        out_specs=(cells, cells, cells, cells),
        check_vma=False,
    )
```

profile of v0, /device:TPU:1, one launch (start us, length us, event | category | flops | bytes accessed | tf_op | source)
XLA Modules:
  0.0 113.6 jit_solution(1328707133518788505)
XLA Ops:
  0.6 0.0 copy-start.9
  0.6 0.0 copy-start.8
  0.7 0.6 copy-done.9
  1.3 0.1 fusion
  1.4 0.0 copy-done.8
  1.4 0.1 reshape.41
  1.5 0.1 broadcast_in_dim.2.listed_ref
  1.6 0.0 copy-start
  1.6 1.0 copy-done
  2.6 0.0 copy-start.1
  2.6 0.9 copy-done.1
  3.5 0.0 copy-start.2
  3.5 0.9 copy-done.2
  4.4 0.0 copy-start.3
  4.4 0.9 copy-done.3
  5.3 0.0 copy-start.4
  5.3 0.9 copy-done.4
  6.1 0.0 copy-start.5
  6.1 0.9 copy-done.5
  7.0 102.5 %shard_map.147 = (bf16[256,1024]{1,0:T(8,128)(2,1)S(1)}, bf16[256,1024]{1,0:T(8,128)(2,1)S(1)}, bf16[256,1024]{1,0:T(8,128)(2,1)}, bf16[256,1024]{1,0:T(8,128)(2,1)}) custom-call(bf16[256,1024]{1,0:T(8,128)(2,1)} %bitcast.14, bf16[256,1024]{1,0:T(8,128)(2,1)} %bitcast.15, bf16[256,1024]{1,0:T(8,128)(2,1)} %bitcast.16, bf16[256,1024]{1,0:T(8,128)(2,1)} %bitcast.17, ...), custom_call_target="tpu_custom_call" | custom-call | flops 4000000000 | bytes 5000000 | tf_op jit(solution)/shard_map/pallas_call | solution.py:407
  109.5 0.8 copy.20
  110.3 0.0 copy-start.7
  110.3 0.8 copy.21
  111.1 0.4 copy-done.7
  111.6 0.0 copy-start.6
  111.6 0.8 copy.22
  112.4 0.4 copy-done.6
  112.8 0.8 copy.23
  (4 shorter events, 0.0 us)
Async XLA Ops:
  0.6 0.7 copy-start.9
  0.6 0.8 copy-start.8
  1.6 1.0 copy-start
  2.6 0.9 copy-start.1
  3.5 0.9 copy-start.2
  4.4 0.9 copy-start.3
  5.3 0.9 copy-start.4
  6.1 0.9 copy-start.5
  110.3 1.2 %copy-start.7 = (bf16[256,1024]{1,0:T(8,128)(2,1)S(1)}, bf16[256,1024]{1,0:T(8,128)(2,1)}, u32[]{:S(2)}) copy-start(bf16[256,1024]{1,0:T(8,128)(2,1)} %get-tuple-element.10) | copy-start | bytes 1572868
  111.6 1.2 %copy-start.6 = (bf16[256,1024]{1,0:T(8,128)(2,1)S(1)}, bf16[256,1024]{1,0:T(8,128)(2,1)}, u32[]{:S(2)}) copy-start(bf16[256,1024]{1,0:T(8,128)(2,1)} %get-tuple-element.11) | copy-start | bytes 1572868
where the time goes:
time: 114 us
  Pallas kernels  102 us (89%)
  local copies, waits for them, and re-layouts  10.3 us (9%)
    pallas_call x1, Pallas kernels, per_device(): pl.pallas_call(functools.partial(kernel, nlon, nlat), out_shape=[jax.Shap...  102 us
    unnamed x24, local copies, waits for them, and re-layouts  10.1 us

commit v1 on v0

--- a/solution.py
+++ b/solution.py
@@ -26,6 +26,10 @@
 KEYS = CORNER + STRIP
 NSLOT = 2 * RANGE + 1
 GROUP = 64
+TURN = 80
+LAG = 2
+PIECES = 3
+WIDE = WCH // PIECES
 GROUPS = CELLS // GROUP
 NEG = -1e30
 SCALE = HEAD**-0.5
@@ -80,7 +84,18 @@
                 at = side * RAD * RAD + c * RAD + r
                 corners[at, side * STRIP + c * SIDE + r] = 1
                 corners[STRIP + at, side * STRIP + c * SIDE + SIDE - RAD + r] = 1
-    return [jnp.asarray(t, BF) for t in (window, axial, strips, strips.T, corners, corners.T)]
+    parts = [np.concatenate([window[0], window[1]], axis=1), axial, strips, strips.T, corners, corners.T]
+    return jnp.asarray(np.concatenate([np.pad(t, ((0, 0), (0, 256 - t.shape[1]))) for t in parts]), BF)
+
+
+class Part:
+    def __init__(self, ref, first, rows, lanes):
+        self.ref, self.first, self.rows, self.lanes = ref, first, rows, lanes
+
+    def read(self, first=0, rows=None, lane=0, lanes=None):
+        start = self.first + first
+        end = start + (self.rows - first if rows is None else rows)
+        return self.ref[start:end, lane:lane + (self.lanes if lanes is None else lanes)]
 
 
 def mm(a, b):
@@ -111,14 +126,27 @@
 
 def kernel(
     nlon, nlat,
-    q_ref, k_ref, v_ref, g_ref, flag_ref, listed_ref,
-    near_ref, row_ref, strips_ref, strips_t_ref, corners_ref, corners_t_ref,
+    q_hbm, k_hbm, v_hbm, g_hbm, table_hbm, flag_ref, listed_ref,
     out_ref, gq_ref, gk_ref, gv_ref,
-    flags, columns, bias, xbias, kv, strip_out, corner_out, xkv,
+    q_ref, k_ref, v_ref, g_ref, table_ref, load_s, flags, columns, bias, xbias, kv, strip_out, corner_out, xkv,
     acc, sides, edge_out, edge_in, side_out, side_in, gx, hop_out, hop_in,
     flag_s, flag_r, strip_s, strip_r, edge_s, edge_r, corner_s, corner_r, ax_s, ax_r,
     bedge_s, bedge_r, bside_s, bside_r, hop_s, hop_r,
 ):
+    loads = [
+        pltpu.make_async_copy(src, dst, load_s.at[i])
+        for i, (src, dst) in enumerate(
+            ((k_hbm, k_ref), (v_hbm, v_ref), (table_hbm, table_ref), (q_hbm, q_ref), (g_hbm, g_ref))
+        )
+    ]
+    for load in loads:
+        load.start()
+    views = []
+    at = 0
+    for rows, lanes in ((KEYS, 256), (NSLOT * GROUP, 128), (2 * STRIP, 256), (CELLS, 192), (2 * STRIP, 192), (2 * STRIP, 192)):
+        views.append(Part(table_ref, at, rows, lanes))
+        at += rows
+    near_ref, row_ref, strips_ref, strips_t_ref, corners_ref, corners_t_ref = views
     lon = lax.axis_index("lon")
     lat = lax.axis_index("lat")
     has_up = lat > 0
@@ -138,19 +166,21 @@
         pl.semaphore_signal(barrier, inc=1, device_id=device(dlon, dlat), device_id_type=pl.DeviceIdType.MESH)
 
     flags[RANGE] = flag_ref[...]
+    for tile, there in enumerate((has_up, has_down)):
+        kv[tile, :, CORNER + TURN:KEYS] = jnp.zeros((2, KEYS - CORNER - TURN, WCH), BF)
+        edge_in[tile, :, STRIP + TURN:] = jnp.zeros((2, STRIP - TURN, WCH), BF)
+
+        @pl.when(jnp.logical_not(there))
+        def _():
+            kv[tile, :, EDGE:CORNER + TURN] = jnp.zeros((2, STRIP + TURN, WCH), BF)
+            edge_in[tile, :, 0:STRIP + TURN] = jnp.zeros((2, STRIP + TURN, WCH), BF)
+
     for part, ref in enumerate((k_ref, v_ref)):
-        cells = ref[:, :WCH]
-        for tile in range(2):
-            kv[tile, part, 0:CELLS] = cells
-        strip_out[part] = mm(strips_ref[...], cells).astype(BF)
+        loads[part].wait()
         for pair in range(XPAIRS):
             at = (2 * pair + part) * PAIR
             xkv[RANGE, :, at:at + PAIR] = ref[:, WCH + pair * PAIR:WCH + (pair + 1) * PAIR]
-    for tile, there in enumerate((has_up, has_down)):
-        @pl.when(jnp.logical_not(there))
-        def _():
-            kv[tile, :, EDGE:KEYS] = jnp.zeros((2, KEYS - EDGE, WCH), BF)
-            edge_in[tile] = jnp.zeros(edge_in.shape[1:], BF)
+        kv[0, part, 0:CELLS] = ref[:, :WCH]
 
     pl.semaphore_wait(barrier, len(NEAR))
 
@@ -159,10 +189,11 @@
         slot = {0: RANGE, -1: 11, 1: 8}[dlat] - dlon
         return remote(flags.at[RANGE], flags.at[slot], flag_s.at[index], flag_r.at[slot], dlon, dlat)
 
-    def strip_copy(way):
-        return remote(
-            strip_out.at[:, pl.ds(way * STRIP, STRIP)], kv.at[0, :, pl.ds(LEFT + way * STRIP, STRIP)],
-            strip_s.at[way], strip_r.at[way], 1 - 2 * way, 0,
+    def strip_copy(way, piece):
+        lanes = pl.ds(piece * WIDE, WIDE)
+        return remote(
+            strip_out.at[:, pl.ds(way * STRIP, STRIP), lanes], kv.at[0, :, pl.ds(LEFT + way * STRIP, STRIP), lanes],
+            strip_s.at[way, piece], strip_r.at[way, piece], 1 - 2 * way, 0,
         )
 
     def edge_copy(way):
@@ -171,23 +202,25 @@
             edge_s.at[way], edge_r.at[way], 0, 2 * way - 1,
         )
 
-    def corner_copy(way):
-        return remote(
-            corner_out.at[:, pl.ds(way * STRIP, STRIP)], kv.at[1 - way, :, pl.ds(CORNER, STRIP)],
-            corner_s.at[way], corner_r.at[way], 0, 2 * way - 1,
-        )
-
-    def ax_copy(way, step):
+    def corner_copy(way, piece):
+        lanes = pl.ds(pl.multiple_of(piece * WIDE, WIDE), WIDE)
+        return remote(
+            corner_out.at[:, pl.ds(way * STRIP, TURN), lanes], kv.at[1 - way, :, pl.ds(CORNER, TURN), lanes],
+            corner_s.at[way, piece], corner_r.at[way, piece], 0, 2 * way - 1,
+        )
+
+    def ax_copy(way, step, pair):
         sign = 1 - 2 * way
-        return remote(
-            xkv.at[RANGE - sign * step], xkv.at[RANGE - sign * (step + 1)],
-            ax_s.at[way, step], ax_r.at[way, step], sign, 0,
+        lanes = pl.ds(pair * 2 * PAIR, 2 * PAIR)
+        return remote(
+            xkv.at[RANGE - sign * step, :, lanes], xkv.at[RANGE - sign * (step + 1), :, lanes],
+            ax_s.at[way, step, pair], ax_r.at[way, step, pair], sign, 0,
         )
 
     def edge_back(way, pair):
         lanes = pl.ds(pl.multiple_of(pair * PAIR, PAIR), PAIR)
         return remote(
-            edge_out.at[way, :, :, lanes], edge_in.at[1 - way, :, :, lanes],
+            edge_out.at[way, :, pl.ds(0, STRIP + TURN), lanes], edge_in.at[1 - way, :, pl.ds(0, STRIP + TURN), lanes],
             bedge_s.at[way, pair], bedge_r.at[way, pair], 0, 2 * way - 1,
         )
 
@@ -215,13 +248,31 @@
         def _():
             make(1 if sending else 0)
 
+    def send_strips(piece):
+        for way in range(2):
+            strip_copy(way, piece).start()
+
+    def turn_strips(piece):
+        lanes = slice(piece * WIDE, (piece + 1) * WIDE)
+        for way in range(2):
+            strip_copy(way, piece).wait_recv()
+        for part in range(2):
+            strip = kv[0, part, LEFT:EDGE, lanes]
+            kv[1, part, LEFT:EDGE, lanes] = strip
+            corner_out[part, :, lanes] = mm(corners_ref.read(), strip).astype(BF)
+        vertical(lambda way: corner_copy(way, piece).start(), True)
+
+    for pair in range(XPAIRS):
+        for way in range(2):
+            ax_copy(way, 0, pair).start()
+    vertical(lambda way: edge_copy(way).start(), True)
     for index in range(len(NEAR)):
         flag_copy(index).start()
-    for way in range(2):
-        strip_copy(way).start()
-    vertical(lambda way: edge_copy(way).start(), True)
-    for way in range(2):
-        ax_copy(way, 0).start()
+    loads[2].wait()
+    for part in range(2):
+        strip_out[part] = mm(strips_ref.read(), kv[0, part, 0:CELLS]).astype(BF)
+    send_strips(0)
+    kv[1, :, 0:CELLS] = kv[0, :, 0:CELLS]
 
     for index in range(len(NEAR)):
         flag_copy(index).wait_recv()
@@ -232,7 +283,7 @@
 
     def sides_of(left, right):
         return jnp.concatenate(
-            [mm(strips_ref[0:STRIP], columns[left]), mm(strips_ref[STRIP:], columns[right])], axis=0
+            [mm(strips_ref.read(0, STRIP), columns[left]), mm(strips_ref.read(STRIP), columns[right])], axis=0
         )
 
     own_flags = columns[RANGE].astype(F32)
@@ -242,10 +293,10 @@
         lives = jnp.where(there, 1.0, 0.0)
         first = CELLS - STRIP if tile == 0 else 0
         edge_flags = columns[base + 1, first:first + STRIP].astype(F32)
-        turn = corners_ref[STRIP:] if tile == 0 else corners_ref[0:STRIP]
+        turn = corners_ref.read(STRIP) if tile == 0 else corners_ref.read(0, STRIP)
         corner_flags = mm(turn, sides_of(base, base + 2).astype(BF))
         serves = jnp.concatenate([own_flags, side_flags, edge_flags * lives, corner_flags * lives], axis=0)
-        bias[tile] = jnp.where(near_ref[tile].astype(F32) + serves > 1.5, 0.0, NEG)
+        bias[tile] = jnp.where(near_ref.read(lane=tile * 128, lanes=128).astype(F32) + serves > 1.5, 0.0, NEG)
     for group in range(GROUPS):
         serves = jnp.concatenate(
             [
@@ -254,17 +305,21 @@
             ],
             axis=0,
         )
-        xbias[group] = jnp.where(row_ref[...].astype(F32) + serves > 1.5, 0.0, NEG)
-
-    for way in range(2):
-        strip_copy(way).wait_recv()
-    for part in range(2):
-        strip = kv[0, part, LEFT:EDGE]
-        kv[1, part, LEFT:EDGE] = strip
-        corner_out[part] = mm(corners_ref[...], strip).astype(BF)
-    vertical(lambda way: corner_copy(way).start(), True)
-    vertical(lambda way: edge_copy(way).wait_recv(), False)
-    vertical(lambda way: corner_copy(way).wait_recv(), False)
+        xbias[group] = jnp.where(row_ref.read().astype(F32) + serves > 1.5, 0.0, NEG)
+
+    def forward(step):
+        for pair in range(XPAIRS):
+            for way in range(2):
+                ax_copy(way, step - 1, pair).wait_recv()
+                ax_copy(way, step, pair).start()
+
+    forward(1)
+    for load in loads[3:]:
+        load.wait()
+    send_strips(1)
+    turn_strips(0)
+    forward(2)
+    send_strips(2)
 
     def send_sides(pair):
         lanes = pl.ds(pl.multiple_of(pair * PAIR, PAIR), PAIR)
@@ -273,12 +328,57 @@
             found = jnp.concatenate(
                 [edge_in[0, part, STRIP:2 * STRIP, lanes], edge_in[1, part, STRIP:2 * STRIP, lanes]], axis=0
             )
-            side_out[part, :, lanes] = (sides[part, :, lanes] + mm(corners_t_ref[...], found)).astype(BF)
+            side_out[part, :, lanes] = (sides[part, :, lanes] + mm(corners_t_ref.read(), found)).astype(BF)
         for way in range(2):
             side_back(way, pair).start()
+
+    def axial_pair(pair):
+        for way in range(2):
+            ax_copy(way, 2, pair).wait_recv()
+        lanes = slice(WCH + pair * PAIR, WCH + (pair + 1) * PAIR)
+        key_lanes = slice(2 * pair * PAIR, (2 * pair + 1) * PAIR)
+        value_lanes = slice((2 * pair + 1) * PAIR, (2 * pair + 2) * PAIR)
+
+        def axial_group(group, carry):
+            cells = pl.ds(pl.multiple_of(group * GROUP, GROUP), GROUP)
+            queries = stacked_heads(q_ref[cells, lanes] * jnp.asarray(SCALE, BF))
+            cotangents = stacked_heads(g_ref[cells, lanes])
+            keys = xkv[:, cells, key_lanes].reshape(NSLOT * GROUP, PAIR)
+            values = xkv[:, cells, value_lanes].reshape(NSLOT * GROUP, PAIR)
+            scores = mm_nt(keys, queries) + xbias[group]
+            probs, dscore = probabilities(scores, mm_nt(values, cotangents))
+            attended = mm_tn(probs, values)
+            grad_q = mm_tn(dscore, keys)
+            low = lax.broadcasted_iota(jnp.int32, (GROUP, PAIR), 1) < HEAD
+            out_ref[cells, lanes] = jnp.where(low, attended[0:GROUP], attended[GROUP:]).astype(BF)
+            gq_ref[cells, lanes] = (jnp.where(low, grad_q[0:GROUP], grad_q[GROUP:]) * SCALE).astype(BF)
+            gx[:, cells, key_lanes] = mm(dscore, queries).reshape(NSLOT, GROUP, PAIR)
+            gx[:, cells, value_lanes] = mm(probs, cotangents).reshape(NSLOT, GROUP, PAIR)
+            return carry
+
+        lax.fori_loop(0, GROUPS, axial_group, 0)
+        both = slice(2 * pair * PAIR, (2 * pair + 2) * PAIR)
+        for way in range(2):
+            hop_out[way, 0, :, both] = gx[2 * RANGE * (1 - way), :, both].astype(BF)
+            hop_back(way, 0, pair).start()
+
+    def hop(step):
+        for pair in range(XPAIRS):
+            both = slice(2 * pair * PAIR, (2 * pair + 2) * PAIR)
+            for way in range(2):
+                slot = 2 * RANGE - step if way == 0 else step
+                hop_back(way, step - 1, pair).wait_recv()
+                total = gx[slot, :, both] + hop_in[way, step - 1, :, both].astype(F32)
+                hop_out[way, step, :, both] = total.astype(BF)
+                hop_back(way, step, pair).start()
 
     def window_pair(pair, carry):
         lanes = pl.ds(pl.multiple_of(pair * PAIR, PAIR), PAIR)
+
+        @pl.when(lax.rem(pair, WIDE // PAIR) == 0)
+        def _():
+            vertical(lambda way: corner_copy(way, pair // (WIDE // PAIR)).wait_recv(), False)
+
         grads = []
         for tile in range(2):
             rows = slice(tile * 128, (tile + 1) * 128)
@@ -303,70 +403,24 @@
             edge_out[1, part, :, lanes] = second[EDGE:].astype(BF)
         vertical(lambda way: edge_back(way, pair).start(), True)
 
-        for step in range(2):
-            @pl.when(pair == 2 * step + 1)
+        for step in range(1, RANGE):
+            @pl.when(pair == 2 * step - 1)
             def _():
-                for way in range(2):
-                    ax_copy(way, step).wait_recv()
-                    ax_copy(way, step + 1).start()
-
-        @pl.when(pair > 0)
+                hop(step)
+
+        @pl.when(pair >= LAG)
         def _():
-            send_sides(pair - 1)
+            send_sides(pair - LAG)
 
         return carry
 
+    for pair in range(XPAIRS):
+        axial_pair(pair)
+        turn_strips(1 + pair)
+    vertical(lambda way: edge_copy(way).wait_recv(), False)
     lax.fori_loop(0, PAIRS, window_pair, 0)
-    send_sides(PAIRS - 1)
-    for way in range(2):
-        ax_copy(way, 2).wait_recv()
-
-    for pair in range(XPAIRS):
-        lanes = slice(WCH + pair * PAIR, WCH + (pair + 1) * PAIR)
-        key_lanes = slice(2 * pair * PAIR, (2 * pair + 1) * PAIR)
-        value_lanes = slice((2 * pair + 1) * PAIR, (2 * pair + 2) * PAIR)
-
-        def axial_group(group, carry):
-            cells = pl.ds(pl.multiple_of(group * GROUP, GROUP), GROUP)
-            queries = stacked_heads(q_ref[cells, lanes] * jnp.asarray(SCALE, BF))
-            cotangents = stacked_heads(g_ref[cells, lanes])
-            keys = xkv[:, cells, key_lanes].reshape(NSLOT * GROUP, PAIR)
-            values = xkv[:, cells, value_lanes].reshape(NSLOT * GROUP, PAIR)
-            scores = mm_nt(keys, queries) + xbias[group]
-            probs, dscore = probabilities(scores, mm_nt(values, cotangents))
-            attended = mm_tn(probs, values)
-            grad_q = mm_tn(dscore, keys)
-            low = lax.broadcasted_iota(jnp.int32, (GROUP, PAIR), 1) < HEAD
-            out_ref[cells, lanes] = jnp.where(low, attended[0:GROUP], attended[GROUP:]).astype(BF)
-            gq_ref[cells, lanes] = (jnp.where(low, grad_q[0:GROUP], grad_q[GROUP:]) * SCALE).astype(BF)
-            gx[:, cells, key_lanes] = mm(dscore, queries).reshape(NSLOT, GROUP, PAIR)
-            gx[:, cells, value_lanes] = mm(probs, cotangents).reshape(NSLOT, GROUP, PAIR)
-            return carry
-
-        lax.fori_loop(0, GROUPS, axial_group, 0)
-        both = slice(2 * pair * PAIR, (2 * pair + 2) * PAIR)
-        for way in range(2):
-            hop_out[way, 0, :, both] = gx[2 * RANGE * (1 - way), :, both].astype(BF)
-            hop_back(way, 0, pair).start()
-
-    for step in range(1, RANGE):
-        for pair in range(XPAIRS):
-            both = slice(2 * pair * PAIR, (2 * pair + 2) * PAIR)
-            for way in range(2):
-                slot = 2 * RANGE - step if way == 0 else step
-                hop_back(way, step - 1, pair).wait_recv()
-                total = gx[slot, :, both] + hop_in[way, step - 1, :, both].astype(F32)
-                hop_out[way, step, :, both] = total.astype(BF)
-                hop_back(way, step, pair).start()
-
-    for pair in range(PAIRS):
-        for way in range(2):
-            side_back(way, pair).wait_recv()
-    for part, ref in enumerate((gk_ref, gv_ref)):
-        total = acc[part] + mm(strips_t_ref[...], side_in[part])
-        ref[0:STRIP, :WCH] = (total[0:STRIP] + edge_in[0, part, 0:STRIP].astype(F32)).astype(BF)
-        ref[STRIP:CELLS - STRIP, :WCH] = total[STRIP:CELLS - STRIP].astype(BF)
-        ref[CELLS - STRIP:, :WCH] = (total[CELLS - STRIP:] + edge_in[1, part, 0:STRIP].astype(F32)).astype(BF)
+    for late in range(LAG):
+        send_sides(PAIRS - LAG + late)
 
     for pair in range(XPAIRS):
         lanes = slice(WCH + pair * PAIR, WCH + (pair + 1) * PAIR)
@@ -379,18 +433,33 @@
                 total = total + hop_in[way, RANGE - 1, :, at].astype(F32)
             ref[:, lanes] = total.astype(BF)
 
+    for piece in range(PIECES):
+        lanes = slice(piece * WIDE, (piece + 1) * WIDE)
+        for pair in range(piece * (WIDE // PAIR), (piece + 1) * (WIDE // PAIR)):
+            for way in range(2):
+                side_back(way, pair).wait_recv()
+        for part, ref in enumerate((gk_ref, gv_ref)):
+            total = acc[part, :, lanes] + mm(strips_t_ref.read(), side_in[part, :, lanes])
+            top = total[0:STRIP] + edge_in[0, part, 0:STRIP, lanes].astype(F32)
+            bottom = total[CELLS - STRIP:] + edge_in[1, part, 0:STRIP, lanes].astype(F32)
+            ref[0:STRIP, lanes] = top.astype(BF)
+            ref[STRIP:CELLS - STRIP, lanes] = total[STRIP:CELLS - STRIP].astype(BF)
+            ref[CELLS - STRIP:, lanes] = bottom.astype(BF)
+
     for index in range(len(NEAR)):
         flag_copy(index).wait_send()
     for way in range(2):
-        strip_copy(way).wait_send()
+        for piece in range(PIECES):
+            strip_copy(way, piece).wait_send()
         for step in range(RANGE):
-            ax_copy(way, step).wait_send()
             for pair in range(XPAIRS):
+                ax_copy(way, step, pair).wait_send()
                 hop_back(way, step, pair).wait_send()
         for pair in range(PAIRS):
             side_back(way, pair).wait_send()
     vertical(lambda way: edge_copy(way).wait_send(), True)
-    vertical(lambda way: corner_copy(way).wait_send(), True)
+    for piece in range(PIECES):
+        vertical(lambda way: corner_copy(way, piece).wait_send(), True)
     for pair in range(PAIRS):
         vertical(lambda way: edge_back(way, pair).wait_send(), True)
 
@@ -402,14 +471,18 @@
     offset = (block_lists[0] - lax.axis_index("lon") + RANGE + nlon) % nlon
     listed = jnp.any(jnp.arange(8)[:, None] == offset[None, :], axis=1)
     listed = jnp.broadcast_to(listed[:, None], (8, 128)).astype(F32)
+    table = tables()
     vmem = pl.BlockSpec(memory_space=pltpu.VMEM)
     dma = lambda *s: pltpu.SemaphoreType.DMA(s)
     outs = pl.pallas_call(
         functools.partial(kernel, nlon, nlat),
         out_shape=[jax.ShapeDtypeStruct((CELLS, shape[-1]), BF)] * 4,
-        in_specs=[vmem] * 12,
+        in_specs=[pl.BlockSpec(memory_space=pltpu.HBM)] * 5 + [vmem] * 2,
         out_specs=[vmem] * 4,
         scratch_shapes=[
+            *[pltpu.VMEM((CELLS, shape[-1]), BF)] * 4,
+            pltpu.VMEM(table.shape, BF),
+            dma(5),
             pltpu.VMEM((13, 8, 128), F32),
             pltpu.VMEM((13, CELLS, 128), BF),
             pltpu.VMEM((2, KEYS, 128), F32),
@@ -427,15 +500,15 @@
             pltpu.VMEM((NSLOT, CELLS, 2 * XPAIRS * PAIR), F32),
             pltpu.VMEM((2, RANGE, CELLS, 2 * XPAIRS * PAIR), BF),
             pltpu.VMEM((2, RANGE, CELLS, 2 * XPAIRS * PAIR), BF),
-            dma(len(NEAR)), dma(13), dma(2), dma(2), dma(2), dma(2), dma(2), dma(2),
-            dma(2, RANGE), dma(2, RANGE), dma(2, PAIRS), dma(2, PAIRS), dma(2, PAIRS), dma(2, PAIRS),
+            dma(len(NEAR)), dma(13), dma(2, PIECES), dma(2, PIECES), dma(2), dma(2), dma(2, PIECES), dma(2, PIECES),
+            dma(2, RANGE, XPAIRS), dma(2, RANGE, XPAIRS), dma(2, PAIRS), dma(2, PAIRS), dma(2, PAIRS), dma(2, PAIRS),
             dma(2, RANGE, XPAIRS), dma(2, RANGE, XPAIRS),
         ],
         compiler_params=pltpu.CompilerParams(
             collective_id=0, has_side_effects=True, vmem_limit_bytes=52 * 1024 * 1024
         ),
         cost_estimate=pl.CostEstimate(flops=4_000_000_000, bytes_accessed=5_000_000, transcendentals=3_000_000),
-    )(*flat, flag, listed, *tables())
+    )(*flat, table, flag, listed)
     return tuple(x.reshape(shape) for x in outs)
 
 

time: 114 us -> 91.6 us (0.80)
  Pallas kernels: 102 us -> 86.2 us
  local copies, waits for them, and re-layouts: 10.3 us -> 4.41 us
    pallas_call x1, Pallas kernels: 102 us -> 86.2 us  [per_device(): pl.pallas_call(functools.partial(kernel, nlon, nlat), out_shape=[jax.Shap...]
    unnamed x24 -> x10, local copies, waits for them, and re-layouts: 10.1 us -> 4.25 us
where the time goes in v1:
time: 91.6 us; the launch traced here: 91.4 us
  Pallas kernels  86.2 us (94%)
  local copies, waits for them, and re-layouts  4.41 us (5%)
    pallas_call x1, Pallas kernels, per_device(): pl.pallas_call(functools.partial(kernel, nlon, nlat), out_shape=[jax.Shap...  86.2 us
    unnamed x10, local copies, waits for them, and re-layouts  4.25 us

profile of v1, /device:TPU:1, one launch (start us, length us, event | category | flops | bytes accessed | tf_op | source)
XLA Modules:
  0.0 91.4 jit_solution(15524149126215636598)
XLA Ops:
  0.6 0.0 copy-start.2
  0.6 0.0 copy-start.1
  0.7 0.6 copy-done.2
  1.3 0.1 fusion
  1.4 0.0 copy-done.1
  1.4 0.1 reshape.41
  1.5 0.1 broadcast_in_dim.2.listed_ref
  1.6 86.2 %shard_map.102 = (bf16[256,1024]{1,0:T(8,128)(2,1)S(1)}, bf16[256,1024]{1,0:T(8,128)(2,1)S(1)}, bf16[256,1024]{1,0:T(8,128)(2,1)S(1)}, bf16[256,1024]{1,0:T(8,128)(2,1)}) custom-call(bf16[256,1024]{1,0:T(8,128)(2,1)} %bitcast.14, bf16[256,1024]{1,0:T(8,128)(2,1)} %bitcast.15, bf16[256,1024]{1,0:T(8,128)(2,1)} %bitcast.16, bf16[256,1024]{1,0:T(8,128)(2,1)} %bitcast.17, ...), custom_call_target="tpu_custom_call" | custom-call | flops 4000000000 | bytes 5000000 | tf_op jit(solution)/shard_map/pallas_call | solution.py:477
  87.8 0.8 copy.15
  88.6 0.8 copy.16
  89.4 0.0 copy-start
  89.4 0.8 copy.17
  90.2 0.4 copy-done
  90.6 0.8 copy.18
  (4 shorter events, 0.0 us)
Async XLA Ops:
  0.6 0.7 copy-start.2
  0.6 0.8 copy-start.1
  89.4 1.2 %copy-start = (bf16[256,1024]{1,0:T(8,128)(2,1)S(1)}, bf16[256,1024]{1,0:T(8,128)(2,1)}, u32[]{:S(2)}) copy-start(bf16[256,1024]{1,0:T(8,128)(2,1)} %get-tuple-element.11) | copy-start | bytes 1572868

commit v2 on v1

--- a/solution.py
+++ b/solution.py
@@ -404,7 +404,7 @@
         vertical(lambda way: edge_back(way, pair).start(), True)
 
         for step in range(1, RANGE):
-            @pl.when(pair == 2 * step - 1)
+            @pl.when(pair == 2 * step)
             def _():
                 hop(step)
 
@@ -462,6 +462,18 @@
         vertical(lambda way: corner_copy(way, piece).wait_send(), True)
     for pair in range(PAIRS):
         vertical(lambda way: edge_back(way, pair).wait_send(), True)
+
+
+def store_kernel(*refs):
+    count = len(refs) // 2
+    sources, targets, done = refs[:count], refs[count:2 * count], refs[-1]
+    copies = [
+        pltpu.make_async_copy(src, dst, done.at[i]) for i, (src, dst) in enumerate(zip(sources, targets))
+    ]
+    for copy in copies:
+        copy.start()
+    for copy in copies:
+        copy.wait()
 
 
 def per_device(nlon, nlat, queries, key_vectors, value_vectors, grad_out, key_mask, block_lists):
@@ -509,7 +521,16 @@
         ),
         cost_estimate=pl.CostEstimate(flops=4_000_000_000, bytes_accessed=5_000_000, transcendentals=3_000_000),
     )(*flat, table, flag, listed)
-    return tuple(x.reshape(shape) for x in outs)
+    stored = pl.pallas_call(
+        store_kernel,
+        out_shape=[jax.ShapeDtypeStruct((CELLS, shape[-1]), BF)] * 4,
+        in_specs=[pl.BlockSpec(memory_space=pl.ANY)] * 4,
+        out_specs=[pl.BlockSpec(memory_space=pltpu.HBM)] * 4,
+        scratch_shapes=[dma(4)],
+        compiler_params=pltpu.CompilerParams(vmem_limit_bytes=1024 * 1024),
+        cost_estimate=pl.CostEstimate(flops=0, bytes_accessed=4_000_000, transcendentals=0),
+    )(*outs)
+    return tuple(x.reshape(shape) for x in stored)
 
 
 def solution(mesh):

time: 91.6 us -> 90 us (0.983)
  local copies, waits for them, and re-layouts: 4.41 us -> 1.83 us
  Pallas kernels: 86.2 us -> 87.2 us
    unnamed x10 -> x6, local copies, waits for them, and re-layouts: 4.25 us -> 1.68 us
    pallas_call x0 -> x1, Pallas kernels: none -> 1.34 us  [per_device(): pl.pallas_call(store_kernel, out_shape=[jax.ShapeDtypeStruct((CELLS, shap...]
where the time goes in v2:
time: 90 us; the launch traced here: 89.8 us
  Pallas kernels  87.2 us (97%)
  local copies, waits for them, and re-layouts  1.83 us (2%)
    pallas_call x1, Pallas kernels, per_device(): pl.pallas_call(functools.partial(kernel, nlon, nlat), out_shape=[jax.Shap...  85.8 us

profile of v2, /device:TPU:1, one launch (start us, length us, event | category | flops | bytes accessed | tf_op | source)
XLA Modules:
  0.0 89.8 jit_solution(3978927085177626768)
XLA Ops:
  0.6 0.0 copy-start.2
  0.6 0.0 copy-start.1
  0.7 0.6 copy-done.2
  1.3 0.1 fusion
  1.4 0.0 copy-done.1
  1.4 0.1 reshape.41
  1.5 0.1 broadcast_in_dim.2.listed_ref
  1.6 85.8 %shard_map.102 = (bf16[256,1024]{1,0:T(8,128)(2,1)S(1)}, bf16[256,1024]{1,0:T(8,128)(2,1)S(1)}, bf16[256,1024]{1,0:T(8,128)(2,1)S(1)}, bf16[256,1024]{1,0:T(8,128)(2,1)}) custom-call(bf16[256,1024]{1,0:T(8,128)(2,1)} %bitcast.10, bf16[256,1024]{1,0:T(8,128)(2,1)} %bitcast.11, bf16[256,1024]{1,0:T(8,128)(2,1)} %bitcast.12, bf16[256,1024]{1,0:T(8,128)(2,1)} %bitcast.13, ...), custom_call_target="tpu_custom_call" | custom-call | flops 4000000000 | bytes 5000000 | tf_op jit(solution)/shard_map/pallas_call | solution.py:489
  87.4 0.0 copy-start
  87.4 1.0 %copy-done = bf16[256,1024]{1,0:T(8,128)(2,1)S(1)} copy-done((bf16[256,1024]{1,0:T(8,128)(2,1)S(1)}, bf16[256,1024]{1,0:T(8,128)(2,1)}, u32[]{:S(2)}) %copy-start) | copy-done | bytes 524312
  88.5 1.3 %shard_map.103 = (bf16[256,1024]{1,0:T(8,128)(2,1)}, bf16[256,1024]{1,0:T(8,128)(2,1)}, bf16[256,1024]{1,0:T(8,128)(2,1)}, bf16[256,1024]{1,0:T(8,128)(2,1)}) custom-call(bf16[256,1024]{1,0:T(8,128)(2,1)S(1)} %get-tuple-element.12.refs_0_, bf16[256,1024]{1,0:T(8,128)(2,1)S(1)} %get-tuple-element.13.refs_1_, bf16[256,1024]{1,0:T(8,128)(2,1)S(1)} %get-tuple-element.14.refs_2_, ...), custom_call_target="tpu_custom_call" | custom-call | bytes 4000000 | tf_op jit(solution)/shard_map/pallas_call | solution.py:524
  (4 shorter events, 0.0 us)
Async XLA Ops:
  0.6 0.7 copy-start.2
  0.6 0.8 copy-start.1
  87.4 1.0 %copy-start = (bf16[256,1024]{1,0:T(8,128)(2,1)S(1)}, bf16[256,1024]{1,0:T(8,128)(2,1)}, u32[]{:S(2)}) copy-start(bf16[256,1024]{1,0:T(8,128)(2,1)} %get-tuple-element.15.refs_3_) | copy-start | bytes 1572868

commit v3 on v2

--- a/solution.py
+++ b/solution.py
@@ -127,7 +127,8 @@
 def kernel(
     nlon, nlat,
     q_hbm, k_hbm, v_hbm, g_hbm, table_hbm, flag_ref, listed_ref,
-    out_ref, gq_ref, gk_ref, gv_ref,
+    out_hbm, gq_hbm, gk_hbm, gv_hbm,
+    out_ref, gq_ref, gk_ref, gv_ref, store_s,
     q_ref, k_ref, v_ref, g_ref, table_ref, load_s, flags, columns, bias, xbias, kv, strip_out, corner_out, xkv,
     acc, sides, edge_out, edge_in, side_out, side_in, gx, hop_out, hop_in,
     flag_s, flag_r, strip_s, strip_r, edge_s, edge_r, corner_s, corner_r, ax_s, ax_r,
@@ -419,6 +420,14 @@
         turn_strips(1 + pair)
     vertical(lambda way: edge_copy(way).wait_recv(), False)
     lax.fori_loop(0, PAIRS, window_pair, 0)
+    stores = [
+        pltpu.make_async_copy(src, dst, store_s.at[i])
+        for i, (src, dst) in enumerate(
+            ((out_ref, out_hbm), (gq_ref, gq_hbm), (gk_ref, gk_hbm), (gv_ref, gv_hbm))
+        )
+    ]
+    for store in stores[:2]:
+        store.start()
     for late in range(LAG):
         send_sides(PAIRS - LAG + late)
 
@@ -445,6 +454,9 @@
             ref[0:STRIP, lanes] = top.astype(BF)
             ref[STRIP:CELLS - STRIP, lanes] = total[STRIP:CELLS - STRIP].astype(BF)
             ref[CELLS - STRIP:, lanes] = bottom.astype(BF)
+
+    for store in stores[2:]:
+        store.start()
 
     for index in range(len(NEAR)):
         flag_copy(index).wait_send()
@@ -462,6 +474,8 @@
         vertical(lambda way: corner_copy(way, piece).wait_send(), True)
     for pair in range(PAIRS):
         vertical(lambda way: edge_back(way, pair).wait_send(), True)
+    for store in stores:
+        store.wait()
 
 
 def store_kernel(*refs):
@@ -490,8 +504,10 @@
         functools.partial(kernel, nlon, nlat),
         out_shape=[jax.ShapeDtypeStruct((CELLS, shape[-1]), BF)] * 4,
         in_specs=[pl.BlockSpec(memory_space=pltpu.HBM)] * 5 + [vmem] * 2,
-        out_specs=[vmem] * 4,
+        out_specs=[pl.BlockSpec(memory_space=pltpu.HBM)] * 4,
         scratch_shapes=[
+            *[pltpu.VMEM((CELLS, shape[-1]), BF)] * 4,
+            dma(4),
             *[pltpu.VMEM((CELLS, shape[-1]), BF)] * 4,
             pltpu.VMEM(table.shape, BF),
             dma(5),
@@ -524,7 +540,7 @@
     stored = pl.pallas_call(
         store_kernel,
         out_shape=[jax.ShapeDtypeStruct((CELLS, shape[-1]), BF)] * 4,
-        in_specs=[pl.BlockSpec(memory_space=pl.ANY)] * 4,
+        in_specs=[pl.BlockSpec(memory_space=pltpu.HBM)] * 4,
         out_specs=[pl.BlockSpec(memory_space=pltpu.HBM)] * 4,
         scratch_shapes=[dma(4)],
         compiler_params=pltpu.CompilerParams(vmem_limit_bytes=1024 * 1024),

time: 90 us -> 90 us (level)
  no operation moved by 1% of the time
where the time goes in v3:
time: 90 us; the launch traced here: 89.8 us
  Pallas kernels  87.1 us (97%)
  local copies, waits for them, and re-layouts  1.83 us (2%)
    pallas_call x1, Pallas kernels, per_device(): pl.pallas_call(functools.partial(kernel, nlon, nlat), out_shape=[jax.Shap...  85.8 us

profile of v3, /device:TPU:1, one launch (start us, length us, event | category | flops | bytes accessed | tf_op | source)
XLA Modules:
  0.0 89.8 jit_solution(7661996961835126802)
XLA Ops:
  0.6 0.0 copy-start.2
  0.6 0.0 copy-start.1
  0.7 0.6 copy-done.2
  1.3 0.1 fusion
  1.4 0.0 copy-done.1
  1.4 0.1 reshape.41
  1.5 0.1 broadcast_in_dim.2.listed_ref
  1.6 85.8 %shard_map.102 = (bf16[256,1024]{1,0:T(8,128)(2,1)S(1)}, bf16[256,1024]{1,0:T(8,128)(2,1)S(1)}, bf16[256,1024]{1,0:T(8,128)(2,1)S(1)}, bf16[256,1024]{1,0:T(8,128)(2,1)}) custom-call(bf16[256,1024]{1,0:T(8,128)(2,1)} %bitcast.10, bf16[256,1024]{1,0:T(8,128)(2,1)} %bitcast.11, bf16[256,1024]{1,0:T(8,128)(2,1)} %bitcast.12, bf16[256,1024]{1,0:T(8,128)(2,1)} %bitcast.13, ...), custom_call_target="tpu_custom_call" | custom-call | flops 4000000000 | bytes 5000000 | tf_op jit(solution)/shard_map/pallas_call | solution.py:503
  87.4 0.0 copy-start
  87.4 1.0 %copy-done = bf16[256,1024]{1,0:T(8,128)(2,1)S(1)} copy-done((bf16[256,1024]{1,0:T(8,128)(2,1)S(1)}, bf16[256,1024]{1,0:T(8,128)(2,1)}, u32[]{:S(2)}) %copy-start) | copy-done | bytes 524312
  88.4 1.3 %shard_map.103 = (bf16[256,1024]{1,0:T(8,128)(2,1)}, bf16[256,1024]{1,0:T(8,128)(2,1)}, bf16[256,1024]{1,0:T(8,128)(2,1)}, bf16[256,1024]{1,0:T(8,128)(2,1)}) custom-call(bf16[256,1024]{1,0:T(8,128)(2,1)S(1)} %get-tuple-element.12.refs_0_, bf16[256,1024]{1,0:T(8,128)(2,1)S(1)} %get-tuple-element.13.refs_1_, bf16[256,1024]{1,0:T(8,128)(2,1)S(1)} %get-tuple-element.14.refs_2_, ...), custom_call_target="tpu_custom_call" | custom-call | bytes 4000000 | tf_op jit(solution)/shard_map/pallas_call | solution.py:540
  (4 shorter events, 0.0 us)
Async XLA Ops:
  0.6 0.7 copy-start.2
  0.6 0.8 copy-start.1
  87.4 1.0 %copy-start = (bf16[256,1024]{1,0:T(8,128)(2,1)S(1)}, bf16[256,1024]{1,0:T(8,128)(2,1)}, u32[]{:S(2)}) copy-start(bf16[256,1024]{1,0:T(8,128)(2,1)} %get-tuple-element.15.refs_3_) | copy-start | bytes 1572868
